TPU v7x, 128 devices: a whole 4x4x4 slice. The times are simulated.
128 devices in a mesh: panel: 16 (over y_hi, x, core), snp: 8 (over z, y_lo).
Axes of the slice: x: 4, y: 4 (y_hi: 2, y_lo: 2; y = y_hi * 2 + y_lo), z: 4, core: 2. Of those that a mesh axis runs over, the one named last changes fastest.
Arguments:
- dosage: bfloat16 [32768, 8192], P('panel', 'snp'), may hold values from 0 to 2
- allele_freq: float32 [8192], P('snp'), may hold values from 0.05 to 0.5
- plan: int32 [2, 16], replicated, may hold values from 0 to 15, as said below
Outputs:
- relation: float32 [2, 32768, 2048], P(None, ('panel', 'snp'))
Inputs may be any that keep to these rules, and one draw needn't show every extreme that they name: `plan`: each row pairs the 16 panels into 8 disjoint pairs: no panel meets itself, the partner of a panel's partner is that panel, and no pair meets in two rounds.
All inputs are finite; a program needn't handle non-finite values.
Results may differ from a plain program's by a relative error of at most 0.015.
Values may be sent and summed in bfloat16 or wider, within the bound.
A program may use at most 128 MiB of HBM per device.

v0:
```python
import math

import jax
import jax.numpy as jnp
from jax import lax
from jax.sharding import PartitionSpec as P


def local(dosage, allele_freq, plan):
    deviation = jnp.sqrt(2.0 * allele_freq * (1.0 - allele_freq))
    standard = ((dosage.astype(jnp.float32) - 2.0 * allele_freq) / deviation).astype(jnp.bfloat16)
    panel_count = lax.axis_size("panel")
    slab_total_count = lax.axis_size("snp")
    row_total = standard.shape[0]
    slab_width = standard.shape[1]
    block_row_range = row_total // panel_count
    round_count = plan.shape[0]
    scaling_multiplier = 1.0 / math.sqrt(slab_width * slab_total_count)
    spread = lax.all_to_all(
        standard.reshape(panel_count, block_row_range, slab_width),
        "panel",
        split_axis=0,
        concat_axis=0,
        tiled=True,
    )
    partners = []
    for which_round in range(round_count):
        routed = jnp.take(spread, plan[which_round], axis=0)
        arrived = lax.all_to_all(routed, "panel", split_axis=0, concat_axis=0, tiled=True)
        partners.append(arrived.reshape(row_total, slab_width))
    tiles = []
    for which_round in range(round_count):
        product = lax.dot_general(
            standard,
            partners[which_round],
            (((1,), (1,)), ((), ())),
            preferred_element_type=jnp.float32,
        )
        tiles.append(
            lax.psum_scatter(
                (product * scaling_multiplier).astype(jnp.bfloat16),
                "snp",
                scatter_dimension=0,
                tiled=True,
            ).astype(jnp.float32)
        )
    return jnp.stack(tiles, axis=0)


def solution(mesh):
    return jax.shard_map(
        local,
        mesh=mesh,
        in_specs=(P("panel", "snp"), P("snp"), P()),
        out_specs=P(None, ("panel", "snp"), None),
        check_vma=False,
    )
```

profile of v0, /device:TPU:1, one launch (start us, length us, event | category | flops | bytes accessed | tf_op | source)
XLA Modules:
  0.0 548.8 jit_solution(13790789917471801872)
XLA Ops:
  6.5 0.7 broadcast_multiply_fusion
  7.2 5.5 %divide_convert_fusion = bf16[2048,1024]{1,0:T(8,128)(2,1)} fusion(bf16[2048,1024]{1,0:T(8,128)(2,1)} %param.5, f32[1024]{0:T(1024)S(1)} %get-tuple-element.11, f32[1024]{0:T(1024)S(1)} %get-tuple-element.10), kind=kLoop, calls=%fused_computation.4 | loop fusion | flops 8388608 | bytes 8396800 | tf_op jit(solution)/shard_map/convert_element_type | solution.py:11
  12.7 8.6 %all-to-all-start = ((bf16[16,128,1024]{2,1,0:T(8,128)(2,1)}), bf16[16,128,1024]{2,1,0:T(8,128)(2,1)}, u32[]{:S(2)}, u32[]{:S(2)}) async-start(bf16[16,128,1024]{2,1,0:T(8,128)(2,1)} %bitcast.15), calls=%async_computation | async-start | bytes 8388608 | tf_op jit(solution)/shard_map/all_to_all | solution.py:19
  21.3 0.0 reduce-scatter.3.cloned.1.call-start
  21.3 0.0 copy-done.2
  21.4 55.8 %all-to-all-done = bf16[16,128,1024]{2,1,0:T(8,128)(2,1)} async-done(((bf16[16,128,1024]{2,1,0:T(8,128)(2,1)}), bf16[16,128,1024]{2,1,0:T(8,128)(2,1)}, u32[]{:S(2)}, u32[]{:S(2)}) %all-to-all-start) | async-done | bytes 4194336 | tf_op jit(solution)/shard_map/all_to_all | solution.py:19
  77.2 4.9 gather_fusion
  82.2 2.6 broadcast_select_fusion.1
  84.8 0.0 copy-start
  84.8 57.4 %all_to_all.15 = bf16[16,128,1024]{2,1,0:T(8,128)(2,1)S(1)} all-to-all(bf16[16,128,1024]{2,1,0:T(8,128)(2,1)S(1)} %broadcast_select_fusion.1), channel_id=1, replica_groups=mesh['panel'=16,'snp'=8] {'panel'}, dimensions={0} | all-to-all | bytes 8388608 | tf_op jit(solution)/shard_map/all_to_all | solution.py:29
  142.2 0.0 copy-done
  142.2 10.9 %multiply_convert_fusion.1 = bf16[2048,2048]{1,0:T(8,128)(2,1)} fusion(bf16[2048,1024]{1,0:T(8,128)(2,1)S(1)} %copy-done, bf16[2048,1024]{1,0:T(8,128)(2,1)S(1)} %bitcast.17), kind=kOutput, calls=%fused_computation.3 | convolution fusion | flops 8598323200 | bytes 16777216 | tf_op jit(solution)/shard_map/dot_general | solution.py:33
  153.1 0.0 reduce-scatter.3.cloned.1.call-update
  153.1 0.0 reduce-scatter.5.cloned.1.call-start
  153.2 4.9 gather_fusion.1
  158.1 2.7 broadcast_select_fusion
  160.8 0.0 copy-start.1
  160.8 65.0 %all_to_all.16 = bf16[16,128,1024]{2,1,0:T(8,128)(2,1)S(1)} all-to-all(bf16[16,128,1024]{2,1,0:T(8,128)(2,1)S(1)} %broadcast_select_fusion), channel_id=1, replica_groups=mesh['panel'=16,'snp'=8] {'panel'}, dimensions={0} | all-to-all | bytes 8388608 | tf_op jit(solution)/shard_map/all_to_all | solution.py:29
  225.8 0.0 copy-done.1
  225.8 10.9 %multiply_convert_fusion = bf16[2048,2048]{1,0:T(8,128)(2,1)} fusion(bf16[2048,1024]{1,0:T(8,128)(2,1)S(1)} %copy-done.1, bf16[2048,1024]{1,0:T(8,128)(2,1)S(1)} %bitcast.16), kind=kOutput, calls=%fused_computation.2 | convolution fusion | flops 8598323200 | bytes 16777216 | tf_op jit(solution)/shard_map/dot_general | solution.py:33
  236.7 0.0 reduce-scatter.5.cloned.1.call-update
  236.7 128.8 %reduce-scatter.3.cloned.1.call-done = bf16[256,2048]{1,0:T(8,128)(2,1)} async-done(((bf16[2048,2048]{1,0:T(8,128)(2,1)}), bf16[256,2048]{1,0:T(8,128)(2,1)}) %reduce-scatter.3.cloned.1.call-update) | async-done | bytes 1048592 | tf_op jit(solution)/shard_map/reduce_scatter | solution.py:40
  365.6 172.6 %reduce-scatter.5.cloned.1.call-done = bf16[256,2048]{1,0:T(8,128)(2,1)} async-done(((bf16[2048,2048]{1,0:T(8,128)(2,1)}), bf16[256,2048]{1,0:T(8,128)(2,1)}) %reduce-scatter.5.cloned.1.call-update) | async-done | bytes 1048592 | tf_op jit(solution)/shard_map/reduce_scatter | solution.py:40
  538.1 3.8 maximum_convert_fusion
  (4 shorter events, 0.0 us)
Async XLA Ops:
  12.7 8.6 %copy-start.2 = (s32[2,16]{1,0:T(2,128)S(1)}, s32[2,16]{1,0:T(2,128)}, u32[]{:S(2)}) copy-start(s32[2,16]{1,0:T(2,128)} %param.7) | copy-start | bytes 388
  12.7 64.5 %all-to-all-start = ((bf16[16,128,1024]{2,1,0:T(8,128)(2,1)}), bf16[16,128,1024]{2,1,0:T(8,128)(2,1)}, u32[]{:S(2)}, u32[]{:S(2)}) async-start(bf16[16,128,1024]{2,1,0:T(8,128)(2,1)} %bitcast.15), calls=%async_computation | async-start | bytes 8388608 | tf_op jit(solution)/shard_map/all_to_all | solution.py:19
  21.3 344.3 %reduce-scatter.3.cloned.1.call-start = ((), (), s32[]{:S(2)}) async-start(), calls=%async_computation.5 | async-start | bytes 9437184 | tf_op jit(solution)/shard_map/reduce_scatter | solution.py:40
  84.8 57.4 %copy-start = (bf16[2048,1024]{1,0:T(8,128)(2,1)S(1)}, bf16[2048,1024]{1,0:T(8,128)(2,1)}, u32[]{:S(2)}) copy-start(bf16[2048,1024]{1,0:T(8,128)(2,1)} %divide_convert_fusion) | copy-start | bytes 12582916
  153.1 385.0 %reduce-scatter.5.cloned.1.call-start = ((), (), s32[]{:S(2)}) async-start(), calls=%async_computation.6 | async-start | bytes 9437184 | tf_op jit(solution)/shard_map/reduce_scatter | solution.py:40
  160.8 65.0 %copy-start.1 = (bf16[2048,1024]{1,0:T(8,128)(2,1)S(1)}, bf16[2048,1024]{1,0:T(8,128)(2,1)}, u32[]{:S(2)}) copy-start(bf16[2048,1024]{1,0:T(8,128)(2,1)} %divide_convert_fusion) | copy-start | bytes 12582916
Sparse Core Ops, SparseCore 0:
  153.2 212.2 reduce-scatter.2
  368.0 170.1 reduce-scatter.4
where the time goes:
time: 549 us
  waiting for transfers between devices  357 us (65%)
  blocking collectives  122 us (22%)
  matrix products  21.8 us (4%)
  other arithmetic  15.4 us (3%)
  between operations  13.5 us (2%)
  local copies, waits for them, and re-layouts  9.9 us (2%)
  starting transfers between devices  8.66 us (2%)
    reduce_scatter x2, waiting for transfers between devices, local(): lax.psum_scatter((product * scaling_multiplier).astype(jnp.bfloat16), 'sn...  301 us
    all_to_all x2, blocking collectives, local(): lax.all_to_all(routed, 'panel', split_axis=0, concat_axis=0, tiled=True)  122 us
    all_to_all x1, waiting for transfers between devices, local(): lax.all_to_all(standard.reshape(panel_count, block_row_range, slab_width)...  55.8 us
    dot_general x2, matrix products, local(): lax.dot_general(standard, partners[which_round], (((1,), (1,)), ((), ()))...  21.8 us
  transfers between devices with their start and end apart: 3, of which 3 were waited for; matrix products, arithmetic and copies ran while one was open for 3% of the time, Pallas kernels for 0%

commit v1 on v0

v1 whole, which is shorter than its diff:
```python
import functools
import math

import jax
import jax.numpy as jnp
from jax import lax
from jax.experimental import pallas as pl
from jax.experimental.pallas import tpu as pltpu
from jax.sharding import PartitionSpec as P

MESH = pl.DeviceIdType.MESH
HALF = 8
ORDER = (2, 6, 4, 3, 7, 5, 1)


def wait_for(ref, sem):
    pltpu.make_async_copy(ref, ref, sem).wait()


def tables(plan_ref, step_ref, low_ref, colour_ref, to_ref, from_ref, rank_ref, n):
    def start(v, carry):
        nxt = plan_ref[1, plan_ref[0, v]]
        step_ref[0, v] = nxt
        low_ref[0, v] = jnp.minimum(v, nxt)
        return carry

    lax.fori_loop(0, n, start, 0)
    for j in range(2):

        def double(v, carry, j=j):
            nxt = step_ref[j, step_ref[j, v]]
            step_ref[j + 1, v] = nxt
            low_ref[j + 1, v] = jnp.minimum(low_ref[j, v], low_ref[j, nxt])
            return carry

        lax.fori_loop(0, n, double, 0)

    def settle(v, carry):
        first, second = plan_ref[0, v], plan_ref[1, v]
        zero = low_ref[2, v] < low_ref[2, first]
        colour_ref[v] = jnp.where(zero, 0, 1)
        from_ref[v] = jnp.where(zero, first, second)
        to_ref[v] = jnp.where(zero, second, first)
        return carry

    lax.fori_loop(0, n, settle, 0)

    def ranks(v, carry):
        a, b = carry
        restart = lax.rem(v, HALF) == 0
        a, b = jnp.where(restart, 0, a), jnp.where(restart, 0, b)
        rank_ref[0, v] = a
        rank_ref[1, v] = b
        mine = lax.div(v, HALF)
        a = a + jnp.where(lax.div(to_ref[v], HALF) != mine, 1, 0)
        b = b + jnp.where(lax.div(from_ref[v], HALF) != mine, 1, 0)
        return a, b

    lax.fori_loop(0, n, ranks, (jnp.int32(0), jnp.int32(0)))


def kernel(
    chunks, crossing, plan_ref, freq_ref, dosage_ref, own_ref, other_ref,
    std, pool, cross_out, arr_out, partner, part, zin, yout, yin, total,
    tout, tpool, tcross_out, tarr_out, tin, held, theld,
    step_ref, low_ref, colour_ref, to_ref, from_ref, rank_ref, slot_ref,
    load_sem, ssem, rsem,
):
    rows = 256 // chunks
    panel, snp = lax.axis_index("panel"), lax.axis_index("snp")
    half, me = lax.div(panel, HALF), lax.rem(panel, HALF)
    base = half * HALF
    z, ylo = lax.div(snp, 2), lax.rem(snp, 2)

    def peer(d):
        return lax.rem(me + d, HALF)

    def slab(d):
        return lax.rem(snp + d, 8)

    def deep(dz):
        return lax.rem(z + dz, 4)

    across = (lax.rem(panel + HALF, 2 * HALF), snp)
    beside = (panel, z * 2 + 1 - ylo)

    def copy(stage, i, src, dst, where):
        pltpu.make_async_remote_copy(
            src_ref=src, dst_ref=dst, send_sem=ssem.at[stage, i], recv_sem=rsem.at[stage, i],
            device_id=where, device_id_type=MESH,
        ).start()

    loads = [
        pltpu.make_async_copy(
            dosage_ref.at[:, pl.ds(i * rows, rows)], std.at[:, pl.ds(i * rows, rows)], load_sem.at[i]
        )
        for i in range(chunks)
    ]
    for load in loads:
        load.start()

    greeted = [(base + peer(d), snp) for d in range(1, 8)]
    greeted += [(base + peer(d), slab(d)) for d in range(1, 8)]
    greeted += [(panel, deep(dz) * 2 + ylo) for dz in (1, 2, 3)]
    greeted += [across, beside]
    barrier = pltpu.get_barrier_semaphore()
    for where in greeted:
        pl.semaphore_signal(barrier, inc=1, device_id=where, device_id_type=MESH)
    pl.semaphore_wait(barrier, len(greeted))

    freq = freq_ref[...]
    shift = 2.0 * freq
    scale = 1.0 / jnp.sqrt(2.0 * freq * (1.0 - freq))

    def span(i):
        return pl.ds(pl.multiple_of(i * rows, rows), rows)

    def spread(i):
        for d in ORDER:
            copy(0, i, std.at[peer(d), span(i)], pool.at[i, me], (base + peer(d), snp))

    def standardize(i, carry):
        pltpu.make_async_copy(
            dosage_ref.at[:, span(i)], std.at[:, span(i)], load_sem.at[i]
        ).wait()

        def one(l, c):
            value = (std[l, span(i), :].astype(jnp.float32) - shift) * scale
            std[l, span(i), :] = value.astype(jnp.bfloat16)
            return c

        lax.fori_loop(0, 8, one, 0)
        pool[i, me] = std[me, span(i), :]

        @pl.when(i < 2)
        def _():
            spread(i)

        return carry

    lax.fori_loop(0, chunks, standardize, 0)

    tables(plan_ref, step_ref, low_ref, colour_ref, to_ref, from_ref, rank_ref, 2 * HALF)
    for kind, (needs, gives) in enumerate(((from_ref, to_ref), (to_ref, from_ref))):

        def slots(j, carry, kind=kind, needs=needs, gives=gives):
            def pick(v, found):
                hit = (rank_ref[kind, base + v] == j) & (lax.div(gives[base + v], HALF) != half)
                return found + jnp.where(hit, v, 0)

            slot_ref[kind, j] = lax.fori_loop(0, HALF, pick, jnp.int32(0))
            source = needs[base + j]
            slot_ref[2 + kind, j] = jnp.where(
                lax.div(source, HALF) == half, lax.rem(source, HALF), HALF + rank_ref[kind, source]
            )
            return carry

        lax.fori_loop(0, HALF, slots, 0)
    origin = lax.rem(to_ref[panel], HALF)
    multiplier = 1.0 / math.sqrt(8192.0)

    def cross(stage, i, buf, keep, out, kind):
        keep[0:HALF] = buf[i, 0:HALF]
        for j in range(crossing):
            out[i, j] = keep[slot_ref[kind, j]]
        copy(stage, i, out.at[i], buf.at[i, pl.ds(HALF, crossing)], across)

    def arrive(stage, i, buf, keep, out, dst, kind):
        keep[...] = buf[i]
        for d in ORDER:
            w = peer(d)
            out[i, w] = keep[slot_ref[2 + kind, w]]
            copy(stage, i, out.at[i, w], dst.at[i, me], (base + w, snp))
        dst[i, me] = keep[slot_ref[2 + kind, me]]

    def step(t, carry):
        def stage(lag, first=0):
            return t - lag, (t >= lag + first) & (t < lag + chunks)

        i0, on = stage(0, 2)

        @pl.when(on)
        def _():
            spread(i0)

        i1, on = stage(1)

        @pl.when(on)
        def _():
            wait_for(pool.at[i1, pl.ds(0, 7)], rsem.at[0, i1])
            cross(1, i1, pool, held, cross_out, 0)

        i2, on = stage(2)

        @pl.when(on)
        def _():
            wait_for(cross_out.at[i2], rsem.at[1, i2])
            arrive(2, i2, pool, held, arr_out, partner, 0)

        i3, on = stage(3)

        @pl.when(on)
        def _():
            wait_for(partner.at[i3, pl.ds(0, 7)], rsem.at[2, i3])
            block = partner[i3].reshape(HALF * rows, 1024)
            for dz in (1, 2, 3, 0):
                owner = deep(dz) * 2
                for y in range(2):
                    product = lax.dot_general(
                        block, std[owner + y], (((1,), (1,)), ((), ())), preferred_element_type=jnp.float32
                    )
                    part[i3, owner + y] = (product * multiplier).astype(jnp.bfloat16)
                if dz:
                    copy(3, i3, part.at[i3, pl.ds(owner, 2)], zin.at[i3, dz - 1], (panel, owner + ylo))

        i4, on = stage(4)

        @pl.when(on)
        def _():
            wait_for(zin.at[i4], rsem.at[3, i4])

            def add(y):
                value = part[i4, z * 2 + y].astype(jnp.float32)
                for s in range(3):
                    value = value + zin[i4, s, y].astype(jnp.float32)
                return value

            yout[i4] = add(1 - ylo).astype(jnp.bfloat16)
            copy(4, i4, yout.at[i4], yin.at[i4], beside)
            total[:, span(i4)] = add(ylo).reshape(HALF, rows, 256)

        i5, on = stage(5)

        @pl.when(on)
        def _():
            wait_for(yin.at[i5], rsem.at[4, i5])
            value = total[:, span(i5)] + yin[i5].astype(jnp.float32).reshape(HALF, rows, 256)
            total[:, span(i5)] = value
            tout[i5] = value.astype(jnp.bfloat16)
            for d in ORDER:
                copy(5, i5, tout.at[i5, slab(d)], tpool.at[i5, me], (base + peer(d), slab(d)))
            tpool[i5, me] = tout[i5, snp]

        i6, on = stage(6)

        @pl.when(on)
        def _():
            wait_for(tpool.at[i6, pl.ds(0, 7)], rsem.at[5, i6])
            cross(6, i6, tpool, theld, tcross_out, 1)

        i7, on = stage(7)

        @pl.when(on)
        def _():
            wait_for(tcross_out.at[i7], rsem.at[6, i7])
            arrive(7, i7, tpool, theld, tarr_out, tin, 1)

        i8, on = stage(8)

        @pl.when(on)
        def _():
            wait_for(tin.at[i8, pl.ds(0, 7)], rsem.at[7, i8])
            theld[0:8] = tin[i8]
            for b in range(8):
                member = lax.rem(snp + origin - b + 8, 8)
                other_ref[span(i8), b * 256 : (b + 1) * 256] = theld[member]

        return carry

    lax.fori_loop(0, chunks + 8, step, 0)

    for b in range(8):
        own_ref[:, b * 256 : (b + 1) * 256] = total[b].T

    def drain(i, carry):
        for stage, ref in enumerate(
            (pool.at[i, pl.ds(0, 7)], cross_out.at[i], partner.at[i, pl.ds(0, 7)], zin.at[i],
             yin.at[i], tpool.at[i, pl.ds(0, 7)], tcross_out.at[i], tin.at[i, pl.ds(0, 7)])
        ):
            wait_for(ref, ssem.at[stage, i])
        return carry

    lax.fori_loop(0, chunks, drain, 0)


def tiles(dosage, freq, plan, chunks, crossing, collective_id):
    rows = 256 // chunks
    bf16 = jnp.bfloat16
    vmem, smem = pltpu.VMEM, pltpu.SMEM
    return pl.pallas_call(
        functools.partial(kernel, chunks, crossing),
        out_shape=(
            jax.ShapeDtypeStruct((256, 2048), jnp.float32),
            jax.ShapeDtypeStruct((256, 2048), bf16),
        ),
        in_specs=[
            pl.BlockSpec(memory_space=smem),
            pl.BlockSpec(memory_space=vmem),
            pl.BlockSpec(memory_space=pl.ANY),
        ],
        out_specs=(pl.BlockSpec(memory_space=vmem), pl.BlockSpec(memory_space=vmem)),
        scratch_shapes=[
            vmem((8, 256, 1024), bf16),
            vmem((chunks, HALF + crossing, rows, 1024), bf16),
            vmem((chunks, crossing, rows, 1024), bf16),
            vmem((chunks, HALF, rows, 1024), bf16),
            vmem((chunks, HALF, rows, 1024), bf16),
            vmem((chunks, 8, HALF * rows, 256), bf16),
            vmem((chunks, 3, 2, HALF * rows, 256), bf16),
            vmem((chunks, HALF * rows, 256), bf16),
            vmem((chunks, HALF * rows, 256), bf16),
            vmem((8, 256, 256), jnp.float32),
            vmem((chunks, 8, rows, 256), bf16),
            vmem((chunks, HALF + crossing, rows, 256), bf16),
            vmem((chunks, crossing, rows, 256), bf16),
            vmem((chunks, HALF, rows, 256), bf16),
            vmem((chunks, HALF, rows, 256), bf16),
            vmem((HALF + crossing, rows, 1024), bf16),
            vmem((HALF + crossing, rows, 256), bf16),
            smem((3, 16), jnp.int32),
            smem((3, 16), jnp.int32),
            smem((16,), jnp.int32),
            smem((16,), jnp.int32),
            smem((16,), jnp.int32),
            smem((2, 16), jnp.int32),
            smem((4, 8), jnp.int32),
            pltpu.SemaphoreType.DMA((chunks,)),
            pltpu.SemaphoreType.DMA((8, chunks)),
            pltpu.SemaphoreType.DMA((8, chunks)),
        ],
        compiler_params=pltpu.CompilerParams(
            collective_id=collective_id, has_side_effects=True, vmem_limit_bytes=60 << 20
        ),
        cost_estimate=pl.CostEstimate(flops=2 * 2048 * 2048 * 1024, bytes_accessed=10 << 20, transcendentals=0),
        name=f"tiles{crossing}",
    )(plan, freq, dosage)


def local(dosage, allele_freq, plan):
    dosage = dosage.reshape(8, 256, 1024)
    freq = allele_freq.reshape(1, 1024)
    own, other = tiles(dosage, freq, plan, 8, 8, 0)
    other = other.astype(jnp.float32)
    first, second = plan[0], plan[1]
    who = jnp.arange(16, dtype=jnp.int32)
    hot = lambda p: p[:, None] == who[None, :]
    take = lambda h, x: jnp.sum(jnp.where(h, x[None, :], 0), axis=1)
    jump = take(hot(first), second)
    low = jnp.minimum(who, jump)
    for _ in range(2):
        jump = take(hot(jump), jump)
        low = jnp.minimum(low, take(hot(jump), low))
    zero = low < take(hot(first), low)
    mine = jnp.sum(jnp.where(who == lax.axis_index("panel"), zero, False).astype(jnp.int32)) > 0
    return jnp.stack([jnp.where(mine, own, other), jnp.where(mine, other, own)], axis=0)


def solution(mesh):
    return jax.shard_map(
        local,
        mesh=mesh,
        in_specs=(P("panel", "snp"), P("snp"), P()),
        out_specs=P(None, ("panel", "snp"), None),
        check_vma=False,
    )
```

time: 549 us -> 193 us (0.35)
  waiting for transfers between devices: 357 us -> 0 us
  Pallas kernels: 0 us -> 185 us
  blocking collectives: 122 us -> 0 us
  matrix products: 21.8 us -> 0 us
  between operations: 13.5 us -> 0.68 us
  other arithmetic: 15.4 us -> 6.23 us
  local copies, waits for them, and re-layouts: 9.9 us -> 0.76 us
  starting transfers between devices: 8.66 us -> 0 us
    reduce_scatter x2 -> x0, waiting for transfers between devices: 301 us -> none  [local(): lax.psum_scatter((product * scaling_multiplier).astype(jnp.bfloat16), 'sn...]
    pallas_call x0 -> x1, Pallas kernels: none -> 185 us  [tiles(): pl.pallas_call(functools.partial(kernel, chunks, crossing), out_shape=(ja...]
    all_to_all x2 -> x0, blocking collectives: 122 us -> none  [local(): lax.all_to_all(routed, 'panel', split_axis=0, concat_axis=0, tiled=True)]
    all_to_all x1 -> x0, waiting for transfers between devices: 55.8 us -> none  [local(): lax.all_to_all(standard.reshape(panel_count, block_row_range, slab_width)...]
    dot_general x2 -> x0, matrix products: 21.8 us -> none  [local(): lax.dot_general(standard, partners[which_round], (((1,), (1,)), ((), ()))...]
    gather x2 -> x0, local copies, waits for them, and re-layouts: 9.88 us -> none  [local(): routed = jnp.take(spread, plan[which_round], axis=0)]
    all_to_all x1 -> x0, starting transfers between devices: 8.58 us -> none  [local(): lax.all_to_all(standard.reshape(panel_count, block_row_range, slab_width)...]
    convert_element_type x1 -> x0, other arithmetic: 5.49 us -> none  [local(): ((dosage.astype(jnp.float32) - 2.0 * allele_freq) / deviation).astype(jnp...]
  transfers between devices with their start and end apart: 3 -> 0, of which waited for: 3 -> 0; matrix products, arithmetic and copies ran while one was open for 3% -> 0% of each run, Pallas kernels for 0% -> 0%
where the time goes in v1:
time: 193 us
  Pallas kernels  185 us (96%)
  other arithmetic  6.23 us (3%)
    pallas_call x1, Pallas kernels, tiles(): pl.pallas_call(functools.partial(kernel, chunks, crossing), out_shape=(ja...  185 us
    another operation x2, other arithmetic, local(): jnp.stack([jnp.where(mine, own, other), jnp.where(mine, other, own)], axi...  4.66 us

profile of v1, /device:TPU:1, one launch (start us, length us, event | category | flops | bytes accessed | tf_op | source)
XLA Modules:
  0.0 193.0 jit_solution(7534262946215748868)
XLA Ops:
  0.0 0.8 slice_bitcast_fusion.1
  0.8 0.2 select_reduce_fusion.5
  0.9 0.2 select_reduce_fusion.4
  1.1 0.2 select_reduce_fusion.2
  1.3 0.2 select_reduce_fusion.1
  1.5 0.2 select_reduce_fusion
  1.7 0.6 fusion.2
  3.0 185.3 %tiles8.1 = (f32[256,2048]{1,0:T(8,128)}, bf16[256,2048]{1,0:T(8,128)(2,1)}) custom-call(s32[2,16]{1,0:T(2,128)} %plan_ref.1, f32[1,1024]{1,0:T(1,128)} %bitcast.11, bf16[8,256,1024]{2,1,0:T(8,128)(2,1)} %bitcast.10), custom_call_target="tpu_custom_call" | custom-call | flops 8589934592 | bytes 10485760 | tf_op jit(solution)/shard_map/tiles8/pallas_call | solution.py:290
  188.4 2.4 %fusion = (f32[1,256,2048]{2,1,0:T(8,128)S(1)}, f32[1,256,2048]{2,1,0:T(8,128)S(1)}) fusion(f32[256,2048]{1,0:T(8,128)} %get-tuple-element.7, bf16[256,2048]{1,0:T(8,128)(2,1)} %get-tuple-element.8, pred[]{:T(512)S(6)} %gt.3), kind=kLoop, calls=%fused_computation.3 | loop fusion | flops 1572864 | bytes 7340033 | tf_op jit(solution)/shard_map/stack | solution.py:355
  190.7 2.3 %pad_maximum_fusion = f32[2,256,2048]{2,1,0:T(8,128)} fusion(f32[1,256,2048]{2,1,0:T(8,128)S(1)} %get-tuple-element.12, f32[1,256,2048]{2,1,0:T(8,128)S(1)} %get-tuple-element.11), kind=kLoop, calls=%fused_computation | loop fusion | flops 1048576 | bytes 8388608 | tf_op jit(solution)/shard_map/stack | solution.py:355
  (3 shorter events, 0.0 us)

commit v2 on v1

v2 whole, which is shorter than its diff:
```python
import functools
import math

import jax
import jax.numpy as jnp
from jax import lax
from jax.experimental import pallas as pl
from jax.experimental.pallas import tpu as pltpu
from jax.sharding import PartitionSpec as P

MESH = pl.DeviceIdType.MESH
CHUNKS = 8
PRE = 0
SEQ=(0,1,2,3,4,5,6,7,8,9,10,11)
LAGS=(0,1,2,3,4,5,6,7,8,9,10)
TG = 2
EARLY = 2
HALF = 8
ORDER = (2, 6, 4, 3, 7, 5, 1)


def wait_for(ref, sem):
    pltpu.make_async_copy(ref, ref, sem).wait()


def tables(plan_ref, step_ref, low_ref, colour_ref, to_ref, from_ref, rank_ref, n):
    def start(v, carry):
        nxt = plan_ref[1, plan_ref[0, v]]
        step_ref[0, v] = nxt
        low_ref[0, v] = jnp.minimum(v, nxt)
        return carry

    lax.fori_loop(0, n, start, 0)
    for j in range(2):

        def double(v, carry, j=j):
            nxt = step_ref[j, step_ref[j, v]]
            step_ref[j + 1, v] = nxt
            low_ref[j + 1, v] = jnp.minimum(low_ref[j, v], low_ref[j, nxt])
            return carry

        lax.fori_loop(0, n, double, 0)

    def settle(v, carry):
        first, second = plan_ref[0, v], plan_ref[1, v]
        zero = low_ref[2, v] < low_ref[2, first]
        colour_ref[v] = jnp.where(zero, 0, 1)
        from_ref[v] = jnp.where(zero, first, second)
        to_ref[v] = jnp.where(zero, second, first)
        return carry

    lax.fori_loop(0, n, settle, 0)

    def ranks(v, carry):
        a, b = carry
        restart = lax.rem(v, HALF) == 0
        a, b = jnp.where(restart, 0, a), jnp.where(restart, 0, b)
        rank_ref[0, v] = a
        rank_ref[1, v] = b
        mine = lax.div(v, HALF)
        a = a + jnp.where(lax.div(to_ref[v], HALF) != mine, 1, 0)
        b = b + jnp.where(lax.div(from_ref[v], HALF) != mine, 1, 0)
        return a, b

    lax.fori_loop(0, n, ranks, (jnp.int32(0), jnp.int32(0)))


def kernel(
    chunks, crossing, plan_ref, freq_ref, dosage_ref, own_ref, other_ref, mine_ref,
    std, pool, cross_out, arr_out, partner, part, zfar, zsum, zin, yout, yin, total,
    tout, tpool, tcross_out, tarr_out, tin, held, theld,
    step_ref, low_ref, colour_ref, to_ref, from_ref, rank_ref, slot_ref,
    load_sem, ssem, rsem,
):
    rows = 256 // chunks
    panel, snp = lax.axis_index("panel"), lax.axis_index("snp")
    half, me = lax.div(panel, HALF), lax.rem(panel, HALF)
    base = half * HALF
    z, ylo = lax.div(snp, 2), lax.rem(snp, 2)

    def peer(d):
        return lax.rem(me + d, HALF)

    def slab(d):
        return lax.rem(snp + d, 8)

    def deep(dz):
        return lax.rem(z + dz, 4)

    across = (lax.rem(panel + HALF, 2 * HALF), snp)
    beside = (panel, z * 2 + 1 - ylo)

    def copy(stage, i, src, dst, where):
        pltpu.make_async_remote_copy(
            src_ref=src, dst_ref=dst, send_sem=ssem.at[stage, i], recv_sem=rsem.at[stage, i],
            device_id=where, device_id_type=MESH,
        ).start()

    greeted = [(base + peer(d), snp) for d in range(1, 8)]
    greeted += [(base + peer(d), slab(d)) for d in range(1, 8)]
    greeted += [(panel, deep(dz) * 2 + ylo) for dz in (1, 3)]
    greeted += [across, beside]
    barrier = pltpu.get_barrier_semaphore()
    for where in greeted:
        pl.semaphore_signal(barrier, inc=1, device_id=where, device_id_type=MESH)
    loads = [
        pltpu.make_async_copy(
            dosage_ref.at[:, pl.ds(i * rows, rows)], std.at[:, pl.ds(i * rows, rows)], load_sem.at[i]
        )
        for i in range(chunks)
    ]
    for load in loads:
        load.start()

    freq = freq_ref[...]
    shift = 2.0 * freq
    scale = 1.0 / jnp.sqrt(2.0 * freq * (1.0 - freq))

    def span(i):
        return pl.ds(pl.multiple_of(i * rows, rows), rows)

    def spread(i):
        for d in ORDER:
            copy(0, i, std.at[peer(d), span(i)], pool.at[i, me], (base + peer(d), snp))

    def standardize(i, carry):
        pltpu.make_async_copy(
            dosage_ref.at[:, span(i)], std.at[:, span(i)], load_sem.at[i]
        ).wait()

        def one(l, c):
            value = (std[l, span(i), :].astype(jnp.float32) - shift) * scale
            std[l, span(i), :] = value.astype(jnp.bfloat16)
            return c

        lax.fori_loop(0, 8, one, 0)
        pool[i, me] = std[me, span(i), :]

        return carry

    tables(plan_ref, step_ref, low_ref, colour_ref, to_ref, from_ref, rank_ref, 2 * HALF)
    for kind, (needs, gives) in enumerate(((from_ref, to_ref), (to_ref, from_ref))):

        def slots(j, carry, kind=kind, needs=needs, gives=gives):
            def pick(v, found):
                hit = (rank_ref[kind, base + v] == j) & (lax.div(gives[base + v], HALF) != half)
                return found + jnp.where(hit, v, 0)

            slot_ref[kind, j] = lax.fori_loop(0, HALF, pick, jnp.int32(0))
            source = needs[base + j]
            slot_ref[2 + kind, j] = jnp.where(
                lax.div(source, HALF) == half, lax.rem(source, HALF), HALF + rank_ref[kind, source]
            )
            return carry

        lax.fori_loop(0, HALF, slots, 0)
    lax.fori_loop(0, EARLY, standardize, 0)
    pl.semaphore_wait(barrier, len(greeted))

    for i in range(EARLY):
        spread(i)
    lax.fori_loop(EARLY, chunks, standardize, 0)

    mine_ref[...] = jnp.full((8, 128), colour_ref[panel], jnp.int32)
    origin = lax.rem(to_ref[panel], HALF)
    multiplier = 1.0 / math.sqrt(8192.0)

    def cross(stage, i, buf, keep, out, kind):
        keep[0:HALF] = buf[i, 0:HALF]
        for j in range(crossing):
            out[i, j] = keep[slot_ref[kind, j]]
        copy(stage, i, out.at[i], buf.at[i, pl.ds(HALF, crossing)], across)

    def arrive(stage, i, buf, keep, out, dst, kind):
        keep[...] = buf[i]
        for d in ORDER:
            w = peer(d)
            out[i, w] = keep[slot_ref[2 + kind, w]]
            copy(stage, i, out.at[i, w], dst.at[i, me], (base + w, snp))
        dst[i, me] = keep[slot_ref[2 + kind, me]]

    def step(t, carry):
        def stage(lag, first=0):
            return t - lag, (t >= lag + first) & (t < lag + chunks)

        def stage0():
            i0 = t + PRE

            @pl.when((i0 >= EARLY) & (i0 < chunks))
            def _():
                spread(i0)

        def stage1():
            i1, on = stage(LAGS[1])

            @pl.when(on)
            def _():
                wait_for(pool.at[i1, pl.ds(0, 7)], rsem.at[0, i1])
                cross(1, i1, pool, held, cross_out, 0)

        def stage2():
            i2, on = stage(LAGS[2])

            @pl.when(on)
            def _():
                wait_for(cross_out.at[i2], rsem.at[1, i2])
                arrive(2, i2, pool, held, arr_out, partner, 0)

        def stage3():
            i3, on = stage(LAGS[3])

            @pl.when(on)
            def _():
                wait_for(partner.at[i3, pl.ds(0, 7)], rsem.at[2, i3])
                block = partner[i3].reshape(HALF * rows, 1024)

                def multiply(owner, y):
                    product = lax.dot_general(
                        block, std[owner * 2 + y], (((1,), (1,)), ((), ())), preferred_element_type=jnp.float32
                    )
                    part[i3, owner * 2 + y] = (product * multiplier).astype(jnp.bfloat16)

                def give(stage, owner, y, dst, to):
                    copy(stage, i3, part.at[i3, owner * 2 + y], dst, (panel, to * 2 + ylo))

                after, before, far = deep(1), deep(3), deep(2)
                multiply(far, 0)
                give(3, far, 0, zfar.at[i3, 0], after)
                multiply(far, 1)
                give(3, far, 1, zfar.at[i3, 1], before)
                multiply(after, 1)
                give(4, after, 1, zin.at[i3, 1], after)
                multiply(before, 0)
                give(4, before, 0, zin.at[i3, 0], before)
                multiply(after, 0)
                multiply(before, 1)
                multiply(z, 0)
                multiply(z, 1)

        def stage4():
            i9, on = stage(LAGS[4])

            @pl.when(on)
            def _():
                wait_for(zfar.at[i9], rsem.at[3, i9])
                for y, to in ((0, deep(1)), (1, deep(3))):
                    value = part[i9, to * 2 + y].astype(jnp.float32) + zfar[i9, y].astype(jnp.float32)
                    zsum[i9, y] = value.astype(jnp.bfloat16)
                    copy(4, i9, zsum.at[i9, y], zin.at[i9, 2 + y], (panel, to * 2 + ylo))

        def stage5():
            i4, on = stage(LAGS[5])

            @pl.when(on)
            def _():
                wait_for(zin.at[i4], rsem.at[4, i4])

                def add(y):
                    return (
                        part[i4, z * 2 + y].astype(jnp.float32)
                        + zin[i4, y].astype(jnp.float32)
                        + zin[i4, 2 + y].astype(jnp.float32)
                    )

                yout[i4] = add(1 - ylo).astype(jnp.bfloat16)
                copy(5, i4, yout.at[i4], yin.at[i4], beside)
                total[:, span(i4)] = add(ylo).reshape(HALF, rows, 256)

        def stage6():
            i5, on = stage(LAGS[6])

            @pl.when(on)
            def _():
                wait_for(yin.at[i5], rsem.at[5, i5])
                value = total[:, span(i5)] + yin[i5].astype(jnp.float32).reshape(HALF, rows, 256)
                total[:, span(i5)] = value
                tout[lax.div(i5, TG), :, pl.ds(pl.multiple_of(lax.rem(i5, TG) * rows, rows), rows)] = value.astype(jnp.bfloat16)

        def group(lag):
            u = t - lag
            return lax.div(u, TG), (u >= 0) & (u < chunks) & (lax.rem(u, TG) == 0)

        def stage7():
            j, on = group(LAGS[7])

            @pl.when(on)
            def _():
                for d in ORDER:
                    copy(6, j, tout.at[j, slab(d)], tpool.at[j, me], (base + peer(d), slab(d)))
                tpool[j, me] = tout[j, snp]

        def stage8():
            j, on = group(LAGS[8])

            @pl.when(on)
            def _():
                wait_for(tpool.at[j, pl.ds(0, 7)], rsem.at[6, j])
                cross(7, j, tpool, theld, tcross_out, 1)

        def stage9():
            j, on = group(LAGS[9])

            @pl.when(on)
            def _():
                wait_for(tcross_out.at[j], rsem.at[7, j])
                arrive(8, j, tpool, theld, tarr_out, tin, 1)

        def stage10():
            j, on = group(LAGS[10])

            @pl.when(on)
            def _():
                wait_for(tin.at[j, pl.ds(0, 7)], rsem.at[8, j])
                theld[0:8] = tin[j]
                for b in range(8):
                    member = lax.rem(snp + origin - b + 8, 8)
                    other_ref[pl.ds(pl.multiple_of(j * TG * rows, TG * rows), TG * rows), b * 256 : (b + 1) * 256] = theld[member]

        def stage11():
            @pl.when(t == chunks + LAGS[6])
            def _():
                for b in range(8):
                    own_ref[:, b * 256 : (b + 1) * 256] = total[b].T

        fns = (stage0, stage1, stage2, stage3, stage4, stage5, stage6, stage7, stage8, stage9, stage10, stage11)
        for q in SEQ:
            fns[q]()
        return carry

    lax.fori_loop(0, chunks + LAGS[10], step, 0)

    def drain(i, carry):
        for stage, ref in enumerate(
            (pool.at[i, pl.ds(0, 7)], cross_out.at[i], partner.at[i, pl.ds(0, 7)], zfar.at[i], zin.at[i],
             yin.at[i])
        ):
            wait_for(ref, ssem.at[stage, i])
        return carry

    lax.fori_loop(0, chunks, drain, 0)

    def tdrain(j, carry):
        for stage, ref in enumerate((tpool.at[j, pl.ds(0, 7)], tcross_out.at[j], tin.at[j, pl.ds(0, 7)])):
            wait_for(ref, ssem.at[6 + stage, j])
        return carry

    lax.fori_loop(0, chunks // TG, tdrain, 0)


def tiles(dosage, freq, plan, chunks, crossing, collective_id):
    rows = 256 // chunks
    bf16 = jnp.bfloat16
    vmem, smem = pltpu.VMEM, pltpu.SMEM
    return pl.pallas_call(
        functools.partial(kernel, chunks, crossing),
        out_shape=(
            jax.ShapeDtypeStruct((256, 2048), jnp.float32),
            jax.ShapeDtypeStruct((256, 2048), bf16),
            jax.ShapeDtypeStruct((8, 128), jnp.int32),
        ),
        in_specs=[
            pl.BlockSpec(memory_space=smem),
            pl.BlockSpec(memory_space=vmem),
            pl.BlockSpec(memory_space=pl.ANY),
        ],
        out_specs=(pl.BlockSpec(memory_space=vmem),) * 3,
        scratch_shapes=[
            vmem((8, 256, 1024), bf16),
            vmem((chunks, HALF + crossing, rows, 1024), bf16),
            vmem((chunks, crossing, rows, 1024), bf16),
            vmem((chunks, HALF, rows, 1024), bf16),
            vmem((chunks, HALF, rows, 1024), bf16),
            vmem((chunks, 8, HALF * rows, 256), bf16),
            vmem((chunks, 2, HALF * rows, 256), bf16),
            vmem((chunks, 2, HALF * rows, 256), bf16),
            vmem((chunks, 4, HALF * rows, 256), bf16),
            vmem((chunks, HALF * rows, 256), bf16),
            vmem((chunks, HALF * rows, 256), bf16),
            vmem((8, 256, 256), jnp.float32),
            vmem((chunks // TG, 8, TG * rows, 256), bf16),
            vmem((chunks // TG, HALF + crossing, TG * rows, 256), bf16),
            vmem((chunks // TG, crossing, TG * rows, 256), bf16),
            vmem((chunks // TG, HALF, TG * rows, 256), bf16),
            vmem((chunks // TG, HALF, TG * rows, 256), bf16),
            vmem((HALF + crossing, rows, 1024), bf16),
            vmem((HALF + crossing, TG * rows, 256), bf16),
            smem((3, 16), jnp.int32),
            smem((3, 16), jnp.int32),
            smem((16,), jnp.int32),
            smem((16,), jnp.int32),
            smem((16,), jnp.int32),
            smem((2, 16), jnp.int32),
            smem((4, 8), jnp.int32),
            pltpu.SemaphoreType.DMA((chunks,)),
            pltpu.SemaphoreType.DMA((9, chunks)),
            pltpu.SemaphoreType.DMA((9, chunks)),
        ],
        compiler_params=pltpu.CompilerParams(
            collective_id=collective_id, has_side_effects=True, vmem_limit_bytes=60 << 20
        ),
        cost_estimate=pl.CostEstimate(flops=2 * 2048 * 2048 * 1024, bytes_accessed=10 << 20, transcendentals=0),
        name=f"tiles{crossing}",
    )(plan, freq, dosage)


def local(dosage, allele_freq, plan):
    dosage = dosage.reshape(8, 256, 1024)
    freq = allele_freq.reshape(1, 1024)
    half = jnp.arange(16, dtype=jnp.int32)[None, :] // HALF
    crossings = jnp.sum((plan // HALF != half).astype(jnp.int32))
    few = functools.partial(tiles, chunks=CHUNKS, crossing=5, collective_id=1)
    every = functools.partial(tiles, chunks=CHUNKS, crossing=8, collective_id=0)
    own, other, colour = lax.cond(crossings <= 20, few, every, dosage, freq, plan)
    first = lax.broadcasted_iota(jnp.int32, (2, 256, 2048), 0) == colour[0, 0]
    return jnp.where(first, own[None], other[None].astype(jnp.float32))


def solution(mesh):
    return jax.shard_map(
        local,
        mesh=mesh,
        in_specs=(P("panel", "snp"), P("snp"), P()),
        out_specs=P(None, ("panel", "snp"), None),
        check_vma=False,
    )
```

time: 193 us -> 161 us (0.83)
  Pallas kernels: 185 us -> 154 us
    pallas_call x1, Pallas kernels: 185 us -> 154 us  [tiles(): pl.pallas_call(functools.partial(kernel, chunks, crossing), out_shape=(ja...]
    another operation x2 -> x0, other arithmetic: 4.66 us -> none  [local(): jnp.stack([jnp.where(mine, own, other), jnp.where(mine, other, own)], axi...]
    select_n x0 -> x2, other arithmetic: none -> 2.75 us  [the longest x1 2.75 us: local(): return jnp.where(first, own[None], other[None].astype(jnp.float32))]
where the time goes in v2:
time: 161 us
  Pallas kernels  154 us (96%)
  other arithmetic  4.95 us (3%)
    pallas_call x1, Pallas kernels, tiles(): pl.pallas_call(functools.partial(kernel, chunks, crossing), out_shape=(ja...  154 us

profile of v2, /device:TPU:1, one launch (start us, length us, event | category | flops | bytes accessed | tf_op | source)
XLA Modules:
  0.0 160.5 jit_solution(16167542199584033177)
XLA Ops:
  0.0 1.3 fusion
  2.0 154.4 %conditional.1 = ((f32[256,2048]{1,0:T(8,128)S(1)}, bf16[256,2048]{1,0:T(8,128)(2,1)S(1)}, s32[8,128]{1,0:T(8,128)S(1)})) conditional(s32[]{:T(128)} %convert_element_type.11, (s32[2,16]{1,0:T(2,128)}, f32[1,1024]{1,0:T(1,128)}, bf16[8,256,1024]{2,1,0:T(8,128)(2,1)}) %tuple.18, (s32[2,16]{1,0:T(2,128)}, f32[1,1024]{1,0:T(1,128)}, ...), branch_computations={%region_1.2_spmd, %region_2.3_spmd} | conditional | flops 8589934592 | bytes 10485768 | solution.py:413
  2.0 154.4 %tiles5.1 = (f32[256,2048]{1,0:T(8,128)S(1)}, bf16[256,2048]{1,0:T(8,128)(2,1)S(1)}, s32[8,128]{1,0:T(8,128)S(1)}) custom-call(s32[2,16]{1,0:T(2,128)} %get-tuple-element.20.plan_ref, f32[1,1024]{1,0:T(1,128)} %get-tuple-element.21.freq_ref, bf16[8,256,1024]{2,1,0:T(8,128)(2,1)} %get-tuple-element.22.dosage_ref), custom_call_target="tpu_custom_call" | custom-call | flops 8589934592 | bytes 10485760 | tf_op jit(solution)/shard_map/cond/branch_1_fun/tiles5/pallas_call | solution.py:354
  156.4 0.5 slice.3
  156.9 0.6 iota_compare_fusion
  157.5 0.2 convert_element_type.12
  157.8 2.7 %broadcast_select_fusion = f32[2,256,2048]{2,1,0:T(8,128)} fusion(f32[256,2048]{1,0:T(8,128)S(1)} %convert_element_type.12, f32[256,2048]{1,0:T(8,128)S(1)} %get-tuple-element.27, pred[2]{0:T(512)(128)(4,1)S(1)} %iota_compare_fusion), kind=kLoop, calls=%fused_computation | loop fusion | flops 1048576 | bytes 8388610 | tf_op jit(solution)/shard_map/jit(_where)/select_n | solution.py:415
  (1 shorter events, 0.0 us)

commit v3 on v2

--- a/solution.py
+++ b/solution.py
@@ -11,12 +11,13 @@
 MESH = pl.DeviceIdType.MESH
 CHUNKS = 8
 PRE = 0
-SEQ=(0,1,2,3,4,5,6,7,8,9,10,11)
-LAGS=(0,1,2,3,4,5,6,7,8,9,10)
+SEQ = (0, 1, 2, 3, 4, 5, 6, 7, 8, 9, 10, 11)
+LAGS = (0, 1, 2, 3, 4, 5, 6, 7, 8, 9, 10)
 TG = 2
 EARLY = 2
+BLOCKS = 2
 HALF = 8
-ORDER = (2, 6, 4, 3, 7, 5, 1)
+ORDER = (1, 7, 3, 5, 2, 6, 4)
 
 
 def wait_for(ref, sem):
@@ -77,12 +78,13 @@
     half, me = lax.div(panel, HALF), lax.rem(panel, HALF)
     base = half * HALF
     z, ylo = lax.div(snp, 2), lax.rem(snp, 2)
+    turn = lax.rem(me, 2)
 
     def peer(d):
-        return lax.rem(me + d, HALF)
+        return lax.rem(me + d + turn * (HALF - 2 * d), HALF)
 
     def slab(d):
-        return lax.rem(snp + d, 8)
+        return lax.rem(snp + d + turn * (8 - 2 * d), 8)
 
     def deep(dz):
         return lax.rem(z + dz, 4)
@@ -403,16 +405,39 @@
     )(plan, freq, dosage)
 
 
+def place(colour_ref, own_ref, other_ref, out_ref):
+    own, other = own_ref[...], other_ref[...].astype(jnp.float32)
+    first = colour_ref[0, 0] == 0
+    out_ref[0] = jnp.where(first, own, other)
+    out_ref[1] = jnp.where(first, other, own)
+
+
 def local(dosage, allele_freq, plan):
     dosage = dosage.reshape(8, 256, 1024)
     freq = allele_freq.reshape(1, 1024)
-    half = jnp.arange(16, dtype=jnp.int32)[None, :] // HALF
-    crossings = jnp.sum((plan // HALF != half).astype(jnp.int32))
-    few = functools.partial(tiles, chunks=CHUNKS, crossing=5, collective_id=1)
-    every = functools.partial(tiles, chunks=CHUNKS, crossing=8, collective_id=0)
-    own, other, colour = lax.cond(crossings <= 20, few, every, dosage, freq, plan)
-    first = lax.broadcasted_iota(jnp.int32, (2, 256, 2048), 0) == colour[0, 0]
-    return jnp.where(first, own[None], other[None].astype(jnp.float32))
+    upper = jnp.arange(2 * HALF, dtype=jnp.int32)[None, :] >= HALF
+    crossings = jnp.sum(((plan >= HALF) != upper).astype(jnp.int32))
+    few, some, every = (
+        functools.partial(tiles, chunks=CHUNKS, crossing=crossing, collective_id=i)
+        for i, crossing in enumerate((5, 6, 8))
+    )
+
+    def more(*operands):
+        return lax.cond(crossings <= 24, some, every, *operands)
+
+    own, other, colour = lax.cond(crossings <= 20, few, more, dosage, freq, plan)
+    return pl.pallas_call(
+        place,
+        out_shape=jax.ShapeDtypeStruct((2, 256, 2048), jnp.float32),
+        grid=(BLOCKS,),
+        in_specs=[
+            pl.BlockSpec(memory_space=pltpu.SMEM),
+            pl.BlockSpec((256 // BLOCKS, 2048), lambda i: (i, 0)),
+            pl.BlockSpec((256 // BLOCKS, 2048), lambda i: (i, 0)),
+        ],
+        out_specs=pl.BlockSpec((2, 256 // BLOCKS, 2048), lambda i: (0, i, 0)),
+        name="place",
+    )(colour, own, other)
 
 
 def solution(mesh):

time: 161 us -> 159 us (0.988)
  other arithmetic: 4.95 us -> 1.32 us
  Pallas kernels: 154 us -> 157 us
    pallas_call x0 -> x1, Pallas kernels: none -> 2.82 us  [local(): pl.pallas_call(place, out_shape=jax.ShapeDtypeStruct((2, 256, 2048), jnp....]
    select_n x2 -> x0, other arithmetic: 2.75 us -> none  [the longest x1 2.75 us: local(): return jnp.where(first, own[None], other[None].astype(jnp.float32))]
where the time goes in v3:
time: 159 us
  Pallas kernels  157 us (99%)
    pallas_call x1, Pallas kernels, tiles(): pl.pallas_call(functools.partial(kernel, chunks, crossing), out_shape=(ja...  154 us

profile of v3, /device:TPU:1, one launch (start us, length us, event | category | flops | bytes accessed | tf_op | source)
XLA Modules:
  0.0 158.5 jit_solution(3261805902788878720)
XLA Ops:
  0.0 1.3 fusion
  2.0 153.7 %conditional.2 = ((f32[256,2048]{1,0:T(8,128)S(1)}, bf16[256,2048]{1,0:T(8,128)(2,1)S(1)}, s32[8,128]{1,0:T(8,128)S(1)})) conditional(s32[]{:T(128)} %convert_element_type.10, (s32[]{:T(128)}, s32[2,16]{1,0:T(2,128)}, f32[1,1024]{1,0:T(1,128)}, bf16[8,256,1024]{2,1,0:T(8,128)(2,1)}) %tuple.29, (s32[2,16]{1,0:T(2,128)}, f32[1,1024]{1,0:T(1,128)}, ...), branch_computations={%region_1.0_spmd, %region_4.0_spmd} | conditional | flops 8589934592 | bytes 10485806 | solution.py:428
  2.0 153.7 %tiles5.1 = (f32[256,2048]{1,0:T(8,128)S(1)}, bf16[256,2048]{1,0:T(8,128)(2,1)S(1)}, s32[8,128]{1,0:T(8,128)S(1)}) custom-call(s32[2,16]{1,0:T(2,128)} %get-tuple-element.41.plan_ref, f32[1,1024]{1,0:T(1,128)} %get-tuple-element.42.freq_ref, bf16[8,256,1024]{2,1,0:T(8,128)(2,1)} %get-tuple-element.43.dosage_ref), custom_call_target="tpu_custom_call" | custom-call | flops 8589934592 | bytes 10485760 | tf_op jit(solution)/shard_map/cond/branch_1_fun/tiles5/pallas_call | solution.py:356
  155.7 2.8 %place.1 = f32[2,256,2048]{2,1,0:T(8,128)} custom-call(s32[8,128]{1,0:T(8,128)S(1)} %get-tuple-element.47.colour_ref, f32[256,2048]{1,0:T(8,128)S(1)} %get-tuple-element.48.own_ref, bf16[256,2048]{1,0:T(8,128)(2,1)S(1)} %get-tuple-element.49.other_ref), custom_call_target="tpu_custom_call" | custom-call | tf_op jit(solution)/shard_map/place/pallas_call | solution.py:429
  (1 shorter events, 0.0 us)

commit v4 on v3

--- a/solution.py
+++ b/solution.py
@@ -12,8 +12,8 @@
 CHUNKS = 8
 PRE = 0
 SEQ = (0, 1, 2, 3, 4, 5, 6, 7, 8, 9, 10, 11)
-LAGS = (0, 1, 2, 3, 4, 5, 6, 7, 8, 9, 10)
-TG = 2
+LAGS = (0, 1, 2, 3, 4, 5, 6, 6, 7, 8, 9)
+TG = 1
 EARLY = 2
 BLOCKS = 2
 HALF = 8

time: 159 us -> 156 us (0.981)
  Pallas kernels: 157 us -> 154 us
    pallas_call x1, Pallas kernels: 154 us -> 151 us  [tiles(): pl.pallas_call(functools.partial(kernel, chunks, crossing), out_shape=(ja...]
where the time goes in v4:
time: 156 us
  Pallas kernels  154 us (99%)
    pallas_call x1, Pallas kernels, tiles(): pl.pallas_call(functools.partial(kernel, chunks, crossing), out_shape=(ja...  151 us

profile of v4, /device:TPU:1, one launch (start us, length us, event | category | flops | bytes accessed | tf_op | source)
XLA Modules:
  0.0 155.7 jit_solution(3501783519132784332)
XLA Ops:
  0.0 1.3 fusion
  2.0 150.9 %conditional.2 = ((f32[256,2048]{1,0:T(8,128)S(1)}, bf16[256,2048]{1,0:T(8,128)(2,1)S(1)}, s32[8,128]{1,0:T(8,128)S(1)})) conditional(s32[]{:T(128)} %convert_element_type.10, (s32[]{:T(128)}, s32[2,16]{1,0:T(2,128)}, f32[1,1024]{1,0:T(1,128)}, bf16[8,256,1024]{2,1,0:T(8,128)(2,1)}) %tuple.29, (s32[2,16]{1,0:T(2,128)}, f32[1,1024]{1,0:T(1,128)}, ...), branch_computations={%region_1.0_spmd, %region_4.0_spmd} | conditional | flops 8589934592 | bytes 10485806 | solution.py:428
  2.0 150.9 %tiles5.1 = (f32[256,2048]{1,0:T(8,128)S(1)}, bf16[256,2048]{1,0:T(8,128)(2,1)S(1)}, s32[8,128]{1,0:T(8,128)S(1)}) custom-call(s32[2,16]{1,0:T(2,128)} %get-tuple-element.41.plan_ref, f32[1,1024]{1,0:T(1,128)} %get-tuple-element.42.freq_ref, bf16[8,256,1024]{2,1,0:T(8,128)(2,1)} %get-tuple-element.43.dosage_ref), custom_call_target="tpu_custom_call" | custom-call | flops 8589934592 | bytes 10485760 | tf_op jit(solution)/shard_map/cond/branch_1_fun/tiles5/pallas_call | solution.py:356
  152.9 2.8 %place.1 = f32[2,256,2048]{2,1,0:T(8,128)} custom-call(s32[8,128]{1,0:T(8,128)S(1)} %get-tuple-element.47.colour_ref, f32[256,2048]{1,0:T(8,128)S(1)} %get-tuple-element.48.own_ref, bf16[256,2048]{1,0:T(8,128)(2,1)S(1)} %get-tuple-element.49.other_ref), custom_call_target="tpu_custom_call" | custom-call | tf_op jit(solution)/shard_map/place/pallas_call | solution.py:429
  (1 shorter events, 0.0 us)

commit v5 on v4

--- a/solution.py
+++ b/solution.py
@@ -11,8 +11,8 @@
 MESH = pl.DeviceIdType.MESH
 CHUNKS = 8
 PRE = 0
-SEQ = (0, 1, 2, 3, 4, 5, 6, 7, 8, 9, 10, 11)
-LAGS = (0, 1, 2, 3, 4, 5, 6, 6, 7, 8, 9)
+SEQ = (0, 1, 2, 4, 3, 5, 6, 7, 8, 9, 10, 11)
+LAGS = (0, 1, 2, 3, 4, 4, 5, 5, 6, 7, 8)
 TG = 1
 EARLY = 2
 BLOCKS = 2

time: 156 us -> 154 us (0.987)
  Pallas kernels: 154 us -> 151 us
    pallas_call x1, Pallas kernels: 151 us -> 149 us  [tiles(): pl.pallas_call(functools.partial(kernel, chunks, crossing), out_shape=(ja...]
where the time goes in v5:
time: 154 us; the launch traced here: 153 us
  Pallas kernels  151 us (98%)
    pallas_call x1, Pallas kernels, tiles(): pl.pallas_call(functools.partial(kernel, chunks, crossing), out_shape=(ja...  149 us

profile of v5, /device:TPU:1, one launch (start us, length us, event | category | flops | bytes accessed | tf_op | source)
XLA Modules:
  0.0 153.4 jit_solution(16353024876746919325)
XLA Ops:
  0.0 1.3 fusion
  2.0 148.6 %conditional.2 = ((f32[256,2048]{1,0:T(8,128)S(1)}, bf16[256,2048]{1,0:T(8,128)(2,1)S(1)}, s32[8,128]{1,0:T(8,128)S(1)})) conditional(s32[]{:T(128)} %convert_element_type.10, (s32[]{:T(128)}, s32[2,16]{1,0:T(2,128)}, f32[1,1024]{1,0:T(1,128)}, bf16[8,256,1024]{2,1,0:T(8,128)(2,1)}) %tuple.29, (s32[2,16]{1,0:T(2,128)}, f32[1,1024]{1,0:T(1,128)}, ...), branch_computations={%region_1.0_spmd, %region_4.0_spmd} | conditional | flops 8589934592 | bytes 10485806 | solution.py:428
  2.0 148.6 %tiles5.1 = (f32[256,2048]{1,0:T(8,128)S(1)}, bf16[256,2048]{1,0:T(8,128)(2,1)S(1)}, s32[8,128]{1,0:T(8,128)S(1)}) custom-call(s32[2,16]{1,0:T(2,128)} %get-tuple-element.41.plan_ref, f32[1,1024]{1,0:T(1,128)} %get-tuple-element.42.freq_ref, bf16[8,256,1024]{2,1,0:T(8,128)(2,1)} %get-tuple-element.43.dosage_ref), custom_call_target="tpu_custom_call" | custom-call | flops 8589934592 | bytes 10485760 | tf_op jit(solution)/shard_map/cond/branch_1_fun/tiles5/pallas_call | solution.py:356
  150.6 2.8 %place.1 = f32[2,256,2048]{2,1,0:T(8,128)} custom-call(s32[8,128]{1,0:T(8,128)S(1)} %get-tuple-element.47.colour_ref, f32[256,2048]{1,0:T(8,128)S(1)} %get-tuple-element.48.own_ref, bf16[256,2048]{1,0:T(8,128)(2,1)S(1)} %get-tuple-element.49.other_ref), custom_call_target="tpu_custom_call" | custom-call | tf_op jit(solution)/shard_map/place/pallas_call | solution.py:429
  (1 shorter events, 0.0 us)

commit v6 on v5

--- a/solution.py
+++ b/solution.py
@@ -11,7 +11,7 @@
 MESH = pl.DeviceIdType.MESH
 CHUNKS = 8
 PRE = 0
-SEQ = (0, 1, 2, 4, 3, 5, 6, 7, 8, 9, 10, 11)
+SEQ = (0, 2, 1, 4, 3, 5, 6, 7, 8, 9, 10, 11)
 LAGS = (0, 1, 2, 3, 4, 4, 5, 5, 6, 7, 8)
 TG = 1
 EARLY = 2

time: 154 us -> 153 us (level)
  no operation moved by 1% of the time
where the time goes in v6:
time: 153 us
  Pallas kernels  151 us (99%)
    pallas_call x1, Pallas kernels, tiles(): pl.pallas_call(functools.partial(kernel, chunks, crossing), out_shape=(ja...  148 us

profile of v6, /device:TPU:1, one launch (start us, length us, event | category | flops | bytes accessed | tf_op | source)
XLA Modules:
  0.0 152.9 jit_solution(13612805971509509594)
XLA Ops:
  0.0 1.3 fusion
  2.0 148.1 %conditional.2 = ((f32[256,2048]{1,0:T(8,128)S(1)}, bf16[256,2048]{1,0:T(8,128)(2,1)S(1)}, s32[8,128]{1,0:T(8,128)S(1)})) conditional(s32[]{:T(128)} %convert_element_type.10, (s32[]{:T(128)}, s32[2,16]{1,0:T(2,128)}, f32[1,1024]{1,0:T(1,128)}, bf16[8,256,1024]{2,1,0:T(8,128)(2,1)}) %tuple.29, (s32[2,16]{1,0:T(2,128)}, f32[1,1024]{1,0:T(1,128)}, ...), branch_computations={%region_1.0_spmd, %region_4.0_spmd} | conditional | flops 8589934592 | bytes 10485806 | solution.py:428
  2.0 148.1 %tiles5.1 = (f32[256,2048]{1,0:T(8,128)S(1)}, bf16[256,2048]{1,0:T(8,128)(2,1)S(1)}, s32[8,128]{1,0:T(8,128)S(1)}) custom-call(s32[2,16]{1,0:T(2,128)} %get-tuple-element.41.plan_ref, f32[1,1024]{1,0:T(1,128)} %get-tuple-element.42.freq_ref, bf16[8,256,1024]{2,1,0:T(8,128)(2,1)} %get-tuple-element.43.dosage_ref), custom_call_target="tpu_custom_call" | custom-call | flops 8589934592 | bytes 10485760 | tf_op jit(solution)/shard_map/cond/branch_1_fun/tiles5/pallas_call | solution.py:356
  150.1 2.8 %place.1 = f32[2,256,2048]{2,1,0:T(8,128)} custom-call(s32[8,128]{1,0:T(8,128)S(1)} %get-tuple-element.47.colour_ref, f32[256,2048]{1,0:T(8,128)S(1)} %get-tuple-element.48.own_ref, bf16[256,2048]{1,0:T(8,128)(2,1)S(1)} %get-tuple-element.49.other_ref), custom_call_target="tpu_custom_call" | custom-call | tf_op jit(solution)/shard_map/place/pallas_call | solution.py:429
  (1 shorter events, 0.0 us)
